TPU v7x, 512 devices: a whole 4x8x8 slice. The times are simulated.
512 devices in a mesh: section: 8 (over y_hi, x), expert: 16 (over z, core), dp: 4 (over y_lo).
Axes of the slice: x: 4, y: 8 (y_hi: 2, y_lo: 4; y = y_hi * 4 + y_lo), z: 8, core: 2. Of those that a mesh axis runs over, the one named last changes fastest.
Arguments:
- act: bfloat16 [8, 8192, 3584], P('section', ('expert', 'dp')), may hold values from -6 to 6
- cotangent: bfloat16 [8, 8192, 3584], P('section', ('expert', 'dp')), may hold values from -6 to 6
- expert_ids: int32 [8, 8192, 8], P('section', ('expert', 'dp')), may hold values from 0 to 255, as said below
- gate_values: float32 [8, 8192, 8], P('section', ('expert', 'dp')), may hold values from 0.05 to 0.5
- w_gate: bfloat16 [8, 3584, 2048], P('section', 'dp', 'expert'), may hold values from -0.09375 to 0.09375
- w_up: bfloat16 [8, 3584, 2048], P('section', 'dp', 'expert'), may hold values from -0.09375 to 0.09375
- w_down_t: bfloat16 [8, 3584, 2048], P('section', 'dp', 'expert'), may hold values from -0.1875 to 0.1875
Outputs:
- next_act: bfloat16 [8, 8192, 3584], P('section', ('expert', 'dp'))
- prev_grad: bfloat16 [8, 8192, 3584], P('section', ('expert', 'dp'))
- grad_gate: bfloat16 [8, 3584, 2048], P('section', 'dp', 'expert')
- grad_up: bfloat16 [8, 3584, 2048], P('section', 'dp', 'expert')
- grad_down_t: bfloat16 [8, 3584, 2048], P('section', 'dp', 'expert')
Inputs may be any that keep to these rules, and one draw needn't show every extreme that they name: `expert_ids`: each row names 8 different experts. In each device's rows (aligned blocks of 128 rows) at most 16 rows name any one expert below 2; for each such expert some section and dp index have every block at exactly 16.
All inputs are finite; a program needn't handle non-finite values.
Results may differ from a plain program's by a relative error of at most 0.013.
Values may be sent and summed in bfloat16 or wider, within the bound.
A program may use at most 64 MiB of HBM per device.

v0:
```python
import jax
import jax.numpy as jnp
from jax import lax
from jax.sharding import PartitionSpec as P

WIN_EXP = 2
CAP = 16


def passed_along(block, axis, distance):
    devices = range(lax.axis_size(axis))
    route = [((i - distance) % len(devices), i) for i in devices]
    return lax.ppermute(block, axis, route)


def right_dot(left, right):
    return lax.dot_general(
        left, right, (((1,), (1,)), ((), ())), preferred_element_type=jnp.float32
    )


def rows_dot(left, right):
    return lax.dot_general(
        left, right, (((0,), (0,)), ((), ())), preferred_element_type=jnp.float32
    )


def activate(pre_gate, pre_up, hidden_grad):
    sig = jax.nn.sigmoid(pre_gate)
    silu_gate = pre_gate * sig
    hidden_act = (silu_gate * pre_up).astype(jnp.bfloat16)
    d_gate = (hidden_grad * pre_up * sig * (1.0 + pre_gate * (1.0 - sig))).astype(jnp.bfloat16)
    d_up = (hidden_grad * silu_gate).astype(jnp.bfloat16)
    return (hidden_act, d_gate, d_up)


def per_device(act, cotangent, expert_ids, gate_values, w_gate, w_up, w_down_t):
    model_width = act.shape[2]
    group_size = lax.axis_size("expert") // WIN_EXP
    x_float = act[0].astype(jnp.float32)
    inv_root = lax.rsqrt(jnp.mean(x_float * x_float, axis=-1, keepdims=True) + 1e-06)
    normed = x_float * inv_root
    rows_in = normed.astype(jnp.bfloat16)
    cot_float = cotangent[0].astype(jnp.float32)
    slot_iota = jnp.arange(CAP, dtype=jnp.int32)
    x_packs, g_packs, gate_list, within_list, routed_list = ([], [], [], [], [])
    for expert in range(WIN_EXP):
        named_rows = expert_ids[0] == expert
        gate_of = jnp.sum(jnp.where(named_rows, gate_values[0], 0.0), axis=-1)
        routed = jnp.any(named_rows, axis=-1)
        within = jnp.cumsum(routed.astype(jnp.int32)) - 1
        picker = ((within[None, :] == slot_iota[:, None]) & routed[None, :]).astype(jnp.bfloat16)
        grad_rows = (gate_of[:, None] * cot_float).astype(jnp.bfloat16)
        x_packs.append(
            jnp.dot(picker, rows_in, preferred_element_type=jnp.float32).astype(jnp.bfloat16)
        )
        g_packs.append(
            jnp.dot(picker, grad_rows, preferred_element_type=jnp.float32).astype(jnp.bfloat16)
        )
        gate_list.append(gate_of)
        within_list.append(within)
        routed_list.append(routed)
    x_send = jnp.repeat(jnp.stack(x_packs), group_size, axis=0)
    g_send = jnp.repeat(jnp.stack(g_packs), group_size, axis=0)
    x_recv, g_recv = (
        lax.all_to_all(x_send, "expert", split_axis=0, concat_axis=0, tiled=True),
        lax.all_to_all(g_send, "expert", split_axis=0, concat_axis=0, tiled=True),
    )
    sources = x_recv.shape[0]
    buffer_rows = sources * CAP
    expert_in = x_recv.reshape(buffer_rows, model_width)
    expert_grad = g_recv.reshape(buffer_rows, model_width)
    stacked = jnp.stack((w_gate[0], w_up[0], w_down_t[0]))
    gathered = lax.all_gather(stacked, "dp", axis=1, tiled=True)
    pre_gate = jnp.dot(expert_in, gathered[0], preferred_element_type=jnp.float32)
    pre_up = jnp.dot(expert_in, gathered[1], preferred_element_type=jnp.float32)
    hidden_grad = jnp.dot(expert_grad, gathered[2], preferred_element_type=jnp.float32)
    hidden_act, d_gate, d_up = activate(pre_gate, pre_up, hidden_grad)
    expert_out = right_dot(hidden_act, gathered[2])
    input_grad = right_dot(d_gate, gathered[0]) + right_dot(d_up, gathered[1])
    grad_terms = jnp.stack(
        (rows_dot(expert_in, d_gate), rows_dot(expert_in, d_up), rows_dot(expert_grad, hidden_act))
    )
    summed = lax.psum_scatter(
        grad_terms.astype(jnp.bfloat16), "dp", scatter_dimension=1, tiled=True
    )
    y_send = expert_out.astype(jnp.bfloat16).reshape(sources, CAP, model_width)
    d_send = input_grad.astype(jnp.bfloat16).reshape(sources, CAP, model_width)
    y_back, d_back = (
        lax.all_to_all(y_send, "expert", split_axis=0, concat_axis=0, tiled=True),
        lax.all_to_all(d_send, "expert", split_axis=0, concat_axis=0, tiled=True),
    )
    y_total = jnp.sum(
        y_back.astype(jnp.float32).reshape(WIN_EXP, group_size, CAP, model_width), axis=1
    )
    d_total = jnp.sum(
        d_back.astype(jnp.float32).reshape(WIN_EXP, group_size, CAP, model_width), axis=1
    )
    combined = jnp.zeros_like(x_float)
    normed_grad = jnp.zeros_like(x_float)
    for expert in range(WIN_EXP):
        picked = jnp.clip(within_list[expert], 0, CAP - 1)
        mask_rows = routed_list[expert][:, None]
        combined = combined + gate_list[expert][:, None] * jnp.where(
            mask_rows, jnp.take(y_total[expert], picked, axis=0), 0.0
        )
        normed_grad = normed_grad + jnp.where(
            mask_rows, jnp.take(d_total[expert], picked, axis=0), 0.0
        )
    section_out = (x_float + combined).astype(jnp.bfloat16)
    spread = jnp.mean(normed * normed_grad, axis=-1, keepdims=True)
    row_grad = (cot_float + inv_root * (normed_grad - normed * spread)).astype(jnp.bfloat16)
    next_act = passed_along(section_out[None], "section", 1)
    prev_grad = passed_along(row_grad[None], "section", -1)
    return (next_act, prev_grad, summed[0][None], summed[1][None], summed[2][None])


def solution(mesh):
    placed = (
        P("section", ("expert", "dp"), None),
        P("section", ("expert", "dp"), None),
        P("section", ("expert", "dp"), None),
        P("section", ("expert", "dp"), None),
        P("section", "dp", "expert"),
        P("section", "dp", "expert"),
        P("section", "dp", "expert"),
    )
    return jax.shard_map(
        per_device,
        mesh=mesh,
        in_specs=placed,
        out_specs=(
            P("section", ("expert", "dp"), None),
            P("section", ("expert", "dp"), None),
            P("section", "dp", "expert"),
            P("section", "dp", "expert"),
            P("section", "dp", "expert"),
        ),
        check_vma=False,
    )
```

profile of v0, /device:TPU:6, one launch (start us, length us, event | category | flops | bytes accessed | tf_op | source)
XLA Modules:
  0.0 303.5 jit_solution(6570951465341026728)
XLA Ops:
  7.2 0.8 select_reduce_fusion.1
  8.0 0.1 copy.14
  8.1 0.2 reduce-window.14
  8.4 1.5 fusion.14
  10.0 0.2 reduce-window.15
  10.3 1.5 fusion.4
  11.8 0.3 fusion.5
  12.2 1.4 broadcast_in_dim.68
  13.6 10.6 %all-to-all-start = ((bf16[16,16,3584]{2,1,0:T(8,128)(2,1)}), bf16[16,16,3584]{2,1,0:T(8,128)(2,1)S(1)}, u32[]{:S(2)}, u32[]{:S(2)}) async-start(bf16[16,16,3584]{2,1,0:T(8,128)(2,1)} %bitcast.93), calls=%async_computation | async-start | bytes 3670016 | tf_op jit(solution)/shard_map/all_to_all | solution.py:66
  24.2 0.9 pad_maximum_fusion.1
  25.2 1.5 fusion.6
  26.7 1.5 fusion.7
  28.2 39.4 %all-to-all-done = bf16[16,16,3584]{2,1,0:T(8,128)(2,1)S(1)} async-done(((bf16[16,16,3584]{2,1,0:T(8,128)(2,1)}), bf16[16,16,3584]{2,1,0:T(8,128)(2,1)S(1)}, u32[]{:S(2)}, u32[]{:S(2)}) %all-to-all-start) | async-done | bytes 1835040 | tf_op jit(solution)/shard_map/all_to_all | solution.py:66
  67.7 1.4 broadcast_in_dim.72
  69.1 4.8 %all-to-all-start.2 = ((bf16[16,16,3584]{2,1,0:T(8,128)(2,1)}), bf16[16,16,3584]{2,1,0:T(8,128)(2,1)}, u32[]{:S(2)}, u32[]{:S(2)}) async-start(bf16[16,16,3584]{2,1,0:T(8,128)(2,1)} %bitcast.94), calls=%async_computation.2 | async-start | bytes 3670016 | tf_op jit(solution)/shard_map/all_to_all | solution.py:67
  73.9 18.4 %all-gather.2.cloned.1.call-done = bf16[3,3584,128]{2,1,0:T(8,128)(2,1)} async-done(((bf16[3,896,128]{2,1,0:T(8,128)(2,1)}), bf16[3,3584,128]{2,1,0:T(8,128)(2,1)}) %all-gather.2.cloned.1.call-update) | async-done | bytes 2752528 | tf_op jit(solution)/shard_map/all_gather | solution.py:74
  92.3 1.8 fusion.32
  94.2 1.8 fusion.33
  96.0 21.6 %all-to-all-done.2 = bf16[16,16,3584]{2,1,0:T(8,128)(2,1)} async-done(((bf16[16,16,3584]{2,1,0:T(8,128)(2,1)}), bf16[16,16,3584]{2,1,0:T(8,128)(2,1)}, u32[]{:S(2)}, u32[]{:S(2)}) %all-to-all-start.2) | async-done | bytes 1835040 | tf_op jit(solution)/shard_map/all_to_all | solution.py:67
  117.5 2.5 multiply_convert_fusion
  120.1 0.6 fusion.31
  120.8 2.0 fusion
  122.7 4.8 %all-to-all-start.3 = ((bf16[16,16,3584]{2,1,0:T(8,128)(2,1)}), bf16[16,16,3584]{2,1,0:T(8,128)(2,1)}, u32[]{:S(2)}, u32[]{:S(2)}) async-start(bf16[16,16,3584]{2,1,0:T(8,128)(2,1)} %bitcast.95), calls=%async_computation.3 | async-start | bytes 3670016 | tf_op jit(solution)/shard_map/all_to_all | solution.py:91
  127.6 3.1 %convolution_convert_fusion = bf16[256,3584]{1,0:T(8,128)(2,1)} fusion(bf16[256,128]{1,0:T(8,128)(2,1)S(1)} %get-tuple-element.25, bf16[3,3584,128]{2,1,0:T(8,128)(2,1)} %all-gather.2.cloned.1.call-done), kind=kOutput, calls=%fused_computation.6 | convolution fusion | flops 235798528 | bytes 2818048 | tf_op jit(solution)/shard_map/dot_general | solution.py:17
  130.7 40.5 %all-to-all-done.3 = bf16[16,16,3584]{2,1,0:T(8,128)(2,1)} async-done(((bf16[16,16,3584]{2,1,0:T(8,128)(2,1)}), bf16[16,16,3584]{2,1,0:T(8,128)(2,1)}, u32[]{:S(2)}, u32[]{:S(2)}) %all-to-all-start.3) | async-done | bytes 1835040 | tf_op jit(solution)/shard_map/all_to_all | solution.py:91
  171.2 4.8 %all-to-all-start.1 = ((bf16[16,16,3584]{2,1,0:T(8,128)(2,1)}), bf16[16,16,3584]{2,1,0:T(8,128)(2,1)}, u32[]{:S(2)}, u32[]{:S(2)}) async-start(bf16[16,16,3584]{2,1,0:T(8,128)(2,1)} %bitcast.92), calls=%async_computation.1 | async-start | bytes 3670016 | tf_op jit(solution)/shard_map/all_to_all | solution.py:90
  176.0 0.2 reduce-scatter.2.cloned.1.call-start
  176.2 2.2 fusion.3
  178.4 0.7 fusion.1
  179.1 0.7 fusion.2
  179.8 1.9 pad_maximum_fusion
  181.8 1.8 convert_reduce_fusion
  183.6 1.3 gather_fusion.2
  184.9 34.7 %all-to-all-done.1 = bf16[16,16,3584]{2,1,0:T(8,128)(2,1)} async-done(((bf16[16,16,3584]{2,1,0:T(8,128)(2,1)}), bf16[16,16,3584]{2,1,0:T(8,128)(2,1)}, u32[]{:S(2)}, u32[]{:S(2)}) %all-to-all-start.1) | async-done | bytes 1835040 | tf_op jit(solution)/shard_map/all_to_all | solution.py:90
  219.6 1.8 convert_reduce_fusion.1
  221.5 2.5 gather_fusion
  223.9 2.5 gather_fusion.3
  226.4 2.4 gather_fusion.1
  228.9 2.3 fusion.11
  231.2 0.5 copy-done.3
  231.7 3.2 %fusion.23 = (bf16[1,128,3584]{2,1,0:T(8,128)(2,1)S(1)}, bf16[1,128,3584]{2,1,0:T(8,128)(2,1)S(1)}) fusion(bf16[1,128,3584]{2,1,0:T(8,128)(2,1)S(1)} %copy-done.2, bf16[1,128,3584]{2,1,0:T(8,128)(2,1)S(1)} %copy-done, f32[128]{0:T(128)S(1)} %broadcast_multiply_fusion, f32[128]{0:T(128)S(1)} %add_rsqrt_fusion, f32[128,3584]{1,0:T(8,128)S(1)} %copy-done.1, ...), kind=kLoop, calls=%fused_computation.49 | loop fusion | flops 10092544 | bytes 11012608 | tf_op jit(solution)/shard_map/broadcast_in_dim | solution.py:114
  234.9 7.7 %collective-permute-start = (bf16[1,128,3584]{2,1,0:T(8,128)(2,1)S(1)}, bf16[1,128,3584]{2,1,0:T(8,128)(2,1)S(1)}, u32[]{:S(2)}, u32[]{:S(2)}) collective-permute-start(bf16[1,128,3584]{2,1,0:T(8,128)(2,1)S(1)} %get-tuple-element.15), channel_id=1, source_target_pairs={{448,0},{0,64},{64,128},{128,192},{192,256},{256,320},{320,384},{3... | collective-permute-start | bytes 2752520 | tf_op jit(solution)/shard_map/ppermute | solution.py:13
  242.6 1.9 collective-permute-start.1
  244.5 37.9 %collective-permute-done = bf16[1,128,3584]{2,1,0:T(8,128)(2,1)S(1)} collective-permute-done((bf16[1,128,3584]{2,1,0:T(8,128)(2,1)S(1)}, bf16[1,128,3584]{2,1,0:T(8,128)(2,1)S(1)}, u32[]{:S(2)}, u32[]{:S(2)}) %collective-permute-start) | collective-permute-done | bytes 917536 | tf_op jit(solution)/shard_map/ppermute | solution.py:13
  282.4 10.4 %collective-permute-done.1 = bf16[1,128,3584]{2,1,0:T(8,128)(2,1)S(1)} collective-permute-done((bf16[1,128,3584]{2,1,0:T(8,128)(2,1)S(1)}, bf16[1,128,3584]{2,1,0:T(8,128)(2,1)S(1)}, u32[]{:S(2)}, u32[]{:S(2)}) %collective-permute-start.1) | collective-permute-done | bytes 917536 | tf_op jit(solution)/shard_map/ppermute | solution.py:13
  292.8 2.0 fusion.52
  294.8 0.9 copy.18
  295.7 0.9 copy.19
  (35 shorter events, 0.7 us)
Async XLA Ops:
  7.2 4.6 %copy-start = (bf16[1,128,3584]{2,1,0:T(8,128)(2,1)S(1)}, bf16[1,128,3584]{2,1,0:T(8,128)(2,1)}, u32[]{:S(2)}) copy-start(bf16[1,128,3584]{2,1,0:T(8,128)(2,1)} %param.9) | copy-start | bytes 2752516
  13.6 10.6 %copy-start.5 = (bf16[1,896,128]{2,1,0:T(8,128)(2,1)S(1)}, bf16[1,896,128]{2,1,0:T(8,128)(2,1)}, u32[]{:S(2)}) copy-start(bf16[1,896,128]{2,1,0:T(8,128)(2,1)} %param.15) | copy-start | bytes 688132
  13.6 10.6 %copy-start.6 = (bf16[1,896,128]{2,1,0:T(8,128)(2,1)S(1)}, bf16[1,896,128]{2,1,0:T(8,128)(2,1)}, u32[]{:S(2)}) copy-start(bf16[1,896,128]{2,1,0:T(8,128)(2,1)} %param.14) | copy-start | bytes 688132
  13.6 10.6 %copy-start.7 = (bf16[1,896,128]{2,1,0:T(8,128)(2,1)S(1)}, bf16[1,896,128]{2,1,0:T(8,128)(2,1)}, u32[]{:S(2)}) copy-start(bf16[1,896,128]{2,1,0:T(8,128)(2,1)} %param.13) | copy-start | bytes 688132
  13.6 54.1 %all-to-all-start = ((bf16[16,16,3584]{2,1,0:T(8,128)(2,1)}), bf16[16,16,3584]{2,1,0:T(8,128)(2,1)S(1)}, u32[]{:S(2)}, u32[]{:S(2)}) async-start(bf16[16,16,3584]{2,1,0:T(8,128)(2,1)} %bitcast.93), calls=%async_computation | async-start | bytes 3670016 | tf_op jit(solution)/shard_map/all_to_all | solution.py:66
  24.2 68.2 %all-gather.2.cloned.1.call-start = ((), (), s32[]{:S(2)}) async-start(), calls=%async_computation.5 | async-start | bytes 3440640 | tf_op jit(solution)/shard_map/all_gather | solution.py:74
  69.1 48.4 %all-to-all-start.2 = ((bf16[16,16,3584]{2,1,0:T(8,128)(2,1)}), bf16[16,16,3584]{2,1,0:T(8,128)(2,1)}, u32[]{:S(2)}, u32[]{:S(2)}) async-start(bf16[16,16,3584]{2,1,0:T(8,128)(2,1)} %bitcast.94), calls=%async_computation.2 | async-start | bytes 3670016 | tf_op jit(solution)/shard_map/all_to_all | solution.py:67
  117.5 2.6 copy-start.4
  122.7 48.4 %all-to-all-start.3 = ((bf16[16,16,3584]{2,1,0:T(8,128)(2,1)}), bf16[16,16,3584]{2,1,0:T(8,128)(2,1)}, u32[]{:S(2)}, u32[]{:S(2)}) async-start(bf16[16,16,3584]{2,1,0:T(8,128)(2,1)} %bitcast.95), calls=%async_computation.3 | async-start | bytes 3670016 | tf_op jit(solution)/shard_map/all_to_all | solution.py:91
  171.2 48.4 %all-to-all-start.1 = ((bf16[16,16,3584]{2,1,0:T(8,128)(2,1)}), bf16[16,16,3584]{2,1,0:T(8,128)(2,1)}, u32[]{:S(2)}, u32[]{:S(2)}) async-start(bf16[16,16,3584]{2,1,0:T(8,128)(2,1)} %bitcast.92), calls=%async_computation.1 | async-start | bytes 3670016 | tf_op jit(solution)/shard_map/all_to_all | solution.py:90
  176.0 116.8 %reduce-scatter.2.cloned.1.call-start = ((), (), s32[]{:S(2)}) async-start(), calls=%async_computation.6 | async-start | bytes 3440640 | tf_op jit(solution)/shard_map/reduce_scatter | solution.py:84
  228.8 2.3 copy-start.1
  228.9 2.4 copy-start.2
  228.9 2.9 copy-start.3
  234.9 47.5 %collective-permute-start = (bf16[1,128,3584]{2,1,0:T(8,128)(2,1)S(1)}, bf16[1,128,3584]{2,1,0:T(8,128)(2,1)S(1)}, u32[]{:S(2)}, u32[]{:S(2)}) collective-permute-start(bf16[1,128,3584]{2,1,0:T(8,128)(2,1)S(1)} %get-tuple-element.15), channel_id=1, source_target_pairs={{448,0},{0,64},{64,128},{128,192},{192,256},{256,320},{320,384},{3... | collective-permute-start | bytes 2752520 | tf_op jit(solution)/shard_map/ppermute | solution.py:13
  242.6 50.2 %collective-permute-start.1 = (bf16[1,128,3584]{2,1,0:T(8,128)(2,1)S(1)}, bf16[1,128,3584]{2,1,0:T(8,128)(2,1)S(1)}, u32[]{:S(2)}, u32[]{:S(2)}) collective-permute-start(bf16[1,128,3584]{2,1,0:T(8,128)(2,1)S(1)} %get-tuple-element.14), channel_id=1, source_target_pairs={{64,0},{128,64},{192,128},{256,192},{320,256},{384,320},{448,384},... | collective-permute-start | bytes 2752520 | tf_op jit(solution)/shard_map/ppermute | solution.py:13
Sparse Core Ops, SparseCore 0:
  27.7 64.6 all-gather.1
  181.8 63.3 reduce-scatter.1
where the time goes:
time: 304 us; the launch traced here: 303 us
  waiting for transfers between devices  203 us (67%)
  starting transfers between devices  34.9 us (11%)
  matrix products  20.3 us (7%)
  local copies, waits for them, and re-layouts  16.3 us (5%)
  other arithmetic  14.9 us (5%)
  between operations  14.3 us (5%)
    ppermute x2, waiting for transfers between devices, passed_along(): return lax.ppermute(block, axis, route)  48.2 us
    all_to_all x1, waiting for transfers between devices, per_device(): lax.all_to_all(d_send, 'expert', split_axis=0, concat_axis=0, tiled=True)  40.5 us
    all_to_all x1, waiting for transfers between devices, per_device(): lax.all_to_all(x_send, 'expert', split_axis=0, concat_axis=0, tiled=True)  39.4 us
    all_to_all x1, waiting for transfers between devices, per_device(): lax.all_to_all(y_send, 'expert', split_axis=0, concat_axis=0, tiled=True)  34.7 us
    all_to_all x1, waiting for transfers between devices, per_device(): lax.all_to_all(g_send, 'expert', split_axis=0, concat_axis=0, tiled=True)  21.6 us
    all_gather x1, waiting for transfers between devices, per_device(): gathered = lax.all_gather(stacked, 'dp', axis=1, tiled=True)  18.4 us
    all_to_all x1, starting transfers between devices, per_device(): lax.all_to_all(x_send, 'expert', split_axis=0, concat_axis=0, tiled=True)  10.6 us
    ppermute x2, starting transfers between devices, passed_along(): return lax.ppermute(block, axis, route)  9.59 us
  transfers between devices with their start and end apart: 8, of which 7 were waited for; matrix products, arithmetic and copies ran while one was open for 12% of the time, Pallas kernels for 0%

commit v1 on v0

v1 whole, which is shorter than its diff:
```python
import functools

import jax
import jax.numpy as jnp
from jax import lax
from jax.experimental import pallas as pl
from jax.experimental.pallas import tpu as pltpu
from jax.sharding import PartitionSpec as P

MESH = pl.DeviceIdType.MESH
EXPERTS = 2
CAP = 16
F32 = jnp.float32
BF16 = jnp.bfloat16


def dot(left, right, left_dim, right_dim, precision=None):
    return lax.dot_general(
        left,
        right,
        (((left_dim,), (right_dim,)), ((), ())),
        preferred_element_type=F32,
        precision=precision,
    )


def kernel(
    act, cot, ids, gates, w_gate, w_up, w_down,
    next_act, prev_grad, d_gate_out, d_up_out, d_down_out,
    wf, pk, rb, xg, picks, pick_prev, pick_next, act_in, cot_in,
    normed, hp, hf, hr, ag, yp, rs, ef, fin, ysend, dsend, yin, din, dw_mine, dw_send, dw_in,
    w_s, w_r, a_s, a_r, sh_s, sh_r, bi_s, bo_s, b_r, p_s, p_r, g_s, g_r,
    di_s, do_s, d_r, e_s, e_r, x_s, x_r, q_s, q_r,
):
    sec, ex, d = lax.axis_index("section"), lax.axis_index("expert"), lax.axis_index("dp")
    z, c = ex // 2, ex % 2
    q, half = z % 4, z // 4
    sgn = 1 - 2 * (q // 2)
    qm = q * (1 - q // 2) + (3 - q) * (q // 2)
    edge = 1 - qm
    is_edge, is_inner = qm == 0, qm == 1
    width = act.shape[1]
    chunk = width // 4
    cols = w_gate.shape[1]

    def z_dev(step):
        return {"expert": lax.rem(z + step + 8, 8) * 2 + c}

    inward, outward = z_dev(sgn), z_dev(-sgn)
    sibling = {"expert": z * 2 + 1 - c}
    dp_dev = [{"dp": lax.rem(d + r + 1, 4)} for r in range(3)]
    sec_next = {"section": lax.rem(sec + 1, 8)}
    sec_prev = {"section": lax.rem(sec + 7, 8)}

    bar = pltpu.get_barrier_semaphore()
    for dev in (inward, outward, sibling, *dp_dev, sec_next, sec_prev):
        pl.semaphore_signal(bar, inc=1, device_id=dev, device_id_type=MESH)
    pl.semaphore_wait(bar, 8)

    pending = []

    def make(src, dst, s, r, dev):
        return pltpu.make_async_remote_copy(
            src_ref=src, dst_ref=dst, send_sem=s, recv_sem=r, device_id=dev, device_id_type=MESH
        )

    def send(src, dst, s, r, dev, pred=None):
        def build():
            return make(src, dst, s, r, dev)

        if pred is None:
            build().start()
        else:
            pl.when(pred)(lambda: build().start())
        pending.append((pred, build))

    def arrived(dst, r, s, dev):
        make(dst, dst, s, r, dev).wait_recv()

    base = [0, 1, -1, 2, -2, 3, -3 + 7 * edge, 4 + edge]
    group = [lax.rem(z + sgn * b + 16, 8) for b in base]

    mine = pl.ds(pl.multiple_of(c * cols, cols), cols)
    for k, w in enumerate((w_gate, w_up, w_down)):
        at = pl.ds(pl.multiple_of(2 * cols * k + c * cols, cols), cols)
        send(w, wf.at[:, at], w_s.at[k], w_r.at[k], sibling)
        wf[:, at] = w[...]

    tokens = act.shape[0]
    upper = (
        lax.broadcasted_iota(jnp.int32, (tokens, tokens), 0)
        <= lax.broadcasted_iota(jnp.int32, (tokens, tokens), 1)
    ).astype(BF16)
    slots = lax.broadcasted_iota(jnp.int32, (CAP, tokens), 0).astype(F32)
    ones = jnp.ones((8, ids.shape[1]), F32)
    slot_gate = []
    for e in range(EXPERTS):
        named = ids[...] == e
        gate_of = dot(ones, jnp.where(named, gates[...], 0.0), 1, 1, lax.Precision.HIGHEST)[0:1]
        routed = dot(ones, jnp.where(named, 1.0, 0.0), 1, 1)
        within = dot(routed.astype(BF16), upper, 1, 0)[0:1] - 1.0
        pick = jnp.where((slots == within) & (routed[0:1] > 0.5), 1.0, 0.0)
        slot_gate.append(jnp.sum(pick * gate_of, axis=1, keepdims=True))
        picks[e * CAP : (e + 1) * CAP] = pick.astype(BF16)
    slot_gates = jnp.concatenate(slot_gate, axis=0)
    x_rows = dot(picks[...], act[...], 1, 0)
    inv_root = lax.rsqrt(jnp.mean(x_rows * x_rows, axis=1, keepdims=True) + 1e-6)
    x_rows = x_rows * inv_root
    normed[...] = x_rows
    x_rows = x_rows.astype(BF16)
    g_rows = (slot_gates * dot(picks[...], cot[...], 1, 0)).astype(BF16)
    for e in range(EXPERTS):
        pk[e, 0] = x_rows[e * CAP : (e + 1) * CAP]
        pk[e, 1] = g_rows[e * CAP : (e + 1) * CAP]

    for r in range(3):
        there = lax.rem(d + r + 1, 4)
        at = pl.ds(pl.multiple_of(there * chunk, 128), chunk)
        send(pk.at[:, :, :, at], rb.at[:, :, d], a_s.at[r], a_r.at[r], dp_dev[r])
    own_at = pl.ds(pl.multiple_of(d * chunk, 128), chunk)
    for e in range(EXPERTS):
        for t in range(2):
            rb[e, t, d] = pk[e, t, :, own_at]
    for r in range(3):
        arrived(rb.at[:, :, lax.rem(d + 3 - r, 4)], a_r.at[r], a_s.at[r], dp_dev[r])

    send(rb.at[1 - half], xg.at[8 + (z - 8) * edge], bo_s.at[8], b_r.at[8 + (z - 8) * edge], outward)
    send(rb.at[half], xg.at[z], bi_s.at[0], b_r.at[z], inward)
    send(rb.at[half], xg.at[z], bo_s.at[0], b_r.at[z], outward, is_inner)

    send(picks, pick_prev, sh_s.at[2], sh_r.at[2], sec_next)
    send(picks, pick_next, sh_s.at[3], sh_r.at[3], sec_prev)
    send(act, act_in, sh_s.at[0], sh_r.at[0], sec_next)
    send(cot, cot_in, sh_s.at[1], sh_r.at[1], sec_prev)

    xg[z] = rb[half]
    for k in range(3):
        at = pl.ds(pl.multiple_of(2 * cols * k + (1 - c) * cols, cols), cols)
        arrived(wf.at[:, at], w_r.at[k], w_s.at[k], sibling)

    hidden = 2 * cols
    rows = 4 * CAP

    def front(j):
        g = group[j]
        if j == 1:
            inner = lax.rem(z + sgn + 8, 8)

            @pl.when(is_edge)
            def _():
                arrived(xg.at[8], b_r.at[8], bo_s.at[9], inward)

            send(xg.at[8], xg.at[inner], bo_s.at[9], b_r.at[inner], outward, is_edge)
        if j > 0:
            arrived(xg.at[g], b_r.at[g], bo_s.at[0], inward)
        if j in (1, 3, 5, 7):
            send(xg.at[g], xg.at[g], bo_s.at[j], b_r.at[g], outward, is_inner)
        elif j in (2, 4):
            send(xg.at[g], xg.at[g], bi_s.at[j], b_r.at[g], inward)
        elif j == 6:
            send(xg.at[g], xg.at[g], bi_s.at[j], b_r.at[g], inward, is_inner)
        x = xg[g, 0].reshape(rows, chunk)
        gr = xg[g, 1].reshape(rows, chunk)
        part = jnp.concatenate(
            [dot(x, wf[:, : 2 * hidden], 1, 0), dot(gr, wf[:, 2 * hidden :], 1, 0)], axis=1
        ).reshape(4, CAP, 3 * hidden)
        hf[j] = part
        hp[j] = part.astype(BF16)
        for r in range(3):
            there = lax.rem(d + r + 1, 4)
            send(hp.at[j, there], hr.at[j, r], p_s.at[j, r], p_r.at[j, r], dp_dev[r])

    def middle(j):
        g = group[j]
        total = hf[j, d]
        for r in range(3):
            arrived(hr.at[j, r], p_r.at[j, r], p_s.at[j, r], dp_dev[r])
            total = total + hr[j, r].astype(F32)
        pre_gate = total[:, :hidden]
        pre_up = total[:, hidden : 2 * hidden]
        hidden_grad = total[:, 2 * hidden :]
        sig = jax.nn.sigmoid(pre_gate)
        silu = pre_gate * sig
        ag[g, d, :, :hidden] = (hidden_grad * pre_up * sig * (1.0 + pre_gate * (1.0 - sig))).astype(BF16)
        ag[g, d, :, hidden : 2 * hidden] = (hidden_grad * silu).astype(BF16)
        ag[g, d, :, 2 * hidden :] = (silu * pre_up).astype(BF16)
        for r in range(3):
            send(ag.at[g, d], ag.at[g, d], g_s.at[j, r], g_r.at[j, r], dp_dev[r])

    def back(j):
        g = group[j]
        for r in range(3):
            arrived(ag.at[g, lax.rem(d + 3 - r, 4)], g_r.at[j, r], g_s.at[j, r], dp_dev[r])
        h = ag[g].reshape(rows, 3 * hidden)
        y = dot(h[:, 2 * hidden :], wf[:, 2 * hidden :], 1, 1)
        dx = dot(h[:, : 2 * hidden], wf[:, : 2 * hidden], 1, 1)
        yp[g, 0] = y.astype(BF16).reshape(4, CAP, chunk)
        yp[g, 1] = dx.astype(BF16).reshape(4, CAP, chunk)
        if j in (1, 3, 5, 6, 7):
            slot = 8 if j == 1 else g
            send(yp.at[g], rs.at[slot], di_s.at[j], d_r.at[slot], inward, is_edge)

    for j in range(8):
        front(j)
        if j >= 1:
            middle(j - 1)
        if j >= 2:
            back(j - 2)
    middle(7)
    back(6)
    back(7)

    def add(g, slot):
        yp[g] = (yp[g].astype(F32) + rs[slot].astype(F32)).astype(BF16)

    def chain(j):
        g = group[j]
        arrived(rs.at[g], d_r.at[g], do_s.at[0], inward)
        add(g, g)

    for j in (1, 3, 2, 5, 4, 7, 6):
        g = group[j]
        if j in (2, 4):
            chain(j)
            send(yp.at[g], rs.at[g], do_s.at[j], d_r.at[g], outward, is_inner)
            slot = 9 if j == 2 else 10
            send(yp.at[g], rs.at[slot], do_s.at[j], d_r.at[slot], outward, is_edge)
        else:
            pl.when(is_inner)(functools.partial(chain, j))
            if j == 6:
                send(yp.at[g], rs.at[g], do_s.at[j], d_r.at[g], outward, is_inner)
            else:
                send(yp.at[g], rs.at[g], di_s.at[j], d_r.at[g], inward, is_inner)

    @pl.when(is_edge)
    def _():
        arrived(rs.at[10], d_r.at[10], do_s.at[0], outward)

    send(rs.at[10], rs.at[9], di_s.at[2], d_r.at[9], inward, is_edge)

    arrived(rs.at[z], d_r.at[z], do_s.at[0], inward)
    add(z, z)

    @pl.when(is_inner)
    def _():
        arrived(rs.at[8], d_r.at[8], do_s.at[0], outward)
        add(z, 8)

    def home(src, e, k):
        for r in range(3):
            there = lax.rem(d + r + 1, 4)
            send(src.at[:, there], fin.at[e, :, :, own_at], e_s.at[k, r], e_r.at[k, r], dp_dev[r])
        fin[e, :, :, own_at] = src[:, d]

    home(yp.at[z], half, 0)
    arrived(rs.at[9], d_r.at[9], do_s.at[0], outward)
    home(rs.at[9], 1 - half, 1)

    h_all = ag[...].reshape(8 * rows, 3 * hidden)
    x_all = xg[0:8, 0].reshape(8 * rows, chunk)
    dw_mine[:, : 2 * hidden] = dot(x_all, h_all[:, : 2 * hidden], 0, 0)
    g_all = xg[0:8, 1].reshape(8 * rows, chunk)
    dw_mine[:, 2 * hidden :] = dot(g_all, h_all[:, 2 * hidden :], 0, 0)
    for k in range(3):
        at = pl.ds(pl.multiple_of(hidden * k + (1 - c) * cols, cols), cols)
        dw_send[k] = dw_mine[:, at].astype(BF16)
        send(dw_send.at[k], dw_in.at[k], q_s.at[k], q_r.at[k], sibling)

    for k, e in ((0, half), (1, 1 - half)):
        for r in range(3):
            there = lax.rem(d + 3 - r, 4)
            at = pl.ds(pl.multiple_of(there * chunk, 128), chunk)
            arrived(fin.at[e, :, :, at], e_r.at[k, r], e_s.at[k, r], dp_dev[r])
    y_rows = fin[:, 0].reshape(EXPERTS * CAP, width).astype(F32)
    ysend[...] = (slot_gates * y_rows).astype(BF16)
    send(ysend, yin, x_s.at[0], x_r.at[0], sec_next)
    d_rows = fin[:, 1].reshape(EXPERTS * CAP, width).astype(F32)
    spread = jnp.mean(normed[...] * d_rows, axis=1, keepdims=True)
    dsend[...] = (inv_root * (d_rows - normed[...] * spread)).astype(BF16)
    send(dsend, din, x_s.at[1], x_r.at[1], sec_prev)

    for k, out in enumerate((d_gate_out, d_up_out, d_down_out)):
        arrived(dw_in.at[k], q_r.at[k], q_s.at[k], sibling)
        at = pl.ds(pl.multiple_of(hidden * k + c * cols, cols), cols)
        out[...] = (dw_mine[:, at] + dw_in[k].astype(F32)).astype(BF16)

    arrived(pick_prev, sh_r.at[2], sh_s.at[2], sec_next)
    arrived(act_in, sh_r.at[0], sh_s.at[0], sec_next)
    arrived(yin, x_r.at[0], x_s.at[0], sec_next)
    next_act[...] = (act_in[...].astype(F32) + dot(pick_prev[...], yin[...], 0, 0)).astype(BF16)
    arrived(pick_next, sh_r.at[3], sh_s.at[3], sec_prev)
    arrived(cot_in, sh_r.at[1], sh_s.at[1], sec_prev)
    arrived(din, x_r.at[1], x_s.at[1], sec_prev)
    prev_grad[...] = (cot_in[...].astype(F32) + dot(pick_next[...], din[...], 0, 0)).astype(BF16)

    for pred, build in pending:
        if pred is None:
            build().wait_send()
        else:
            pl.when(pred)(lambda build=build: build().wait_send())


def per_device(act, cotangent, expert_ids, gate_values, w_gate, w_up, w_down_t):
    tokens, width = act.shape[1:]
    depth, cols = w_gate.shape[1:]
    chunk, hidden = width // 4, 2 * cols
    vmem = pl.BlockSpec(memory_space=pltpu.VMEM)
    dma = pltpu.SemaphoreType.DMA
    slots = EXPERTS * CAP
    outs = pl.pallas_call(
        kernel,
        name="moe_relay",
        out_shape=[
            jax.ShapeDtypeStruct((tokens, width), BF16),
            jax.ShapeDtypeStruct((tokens, width), BF16),
            jax.ShapeDtypeStruct((depth, cols), BF16),
            jax.ShapeDtypeStruct((depth, cols), BF16),
            jax.ShapeDtypeStruct((depth, cols), BF16),
        ],
        in_specs=[vmem] * 7,
        out_specs=[vmem] * 5,
        scratch_shapes=[
            pltpu.VMEM((depth, 3 * hidden), BF16),
            pltpu.VMEM((EXPERTS, 2, CAP, width), BF16),
            pltpu.VMEM((EXPERTS, 2, 4, CAP, chunk), BF16),
            pltpu.VMEM((9, 2, 4, CAP, chunk), BF16),
            pltpu.VMEM((slots, tokens), BF16),
            pltpu.VMEM((slots, tokens), BF16),
            pltpu.VMEM((slots, tokens), BF16),
            pltpu.VMEM((tokens, width), BF16),
            pltpu.VMEM((tokens, width), BF16),
            pltpu.VMEM((slots, width), F32),
            pltpu.VMEM((8, 4, CAP, 3 * hidden), BF16),
            pltpu.VMEM((8, 4, CAP, 3 * hidden), F32),
            pltpu.VMEM((8, 3, CAP, 3 * hidden), BF16),
            pltpu.VMEM((8, 4, CAP, 3 * hidden), BF16),
            pltpu.VMEM((8, 2, 4, CAP, chunk), BF16),
            pltpu.VMEM((11, 2, 4, CAP, chunk), BF16),
            pltpu.VMEM((2, 4, CAP, chunk), BF16),
            pltpu.VMEM((EXPERTS, 2, CAP, width), BF16),
            pltpu.VMEM((slots, width), BF16),
            pltpu.VMEM((slots, width), BF16),
            pltpu.VMEM((slots, width), BF16),
            pltpu.VMEM((slots, width), BF16),
            pltpu.VMEM((depth, 3 * hidden), F32),
            pltpu.VMEM((3, depth, cols), BF16),
            pltpu.VMEM((3, depth, cols), BF16),
            dma((3,)), dma((3,)),
            dma((3,)), dma((3,)),
            dma((4,)), dma((4,)),
            dma((8,)), dma((10,)), dma((9,)),
            dma((8, 3)), dma((8, 3)),
            dma((8, 3)), dma((8, 3)),
            dma((8,)), dma((8,)), dma((11,)),
            dma((2, 3)), dma((2, 3)),
            dma((2,)), dma((2,)),
            dma((3,)), dma((3,)),
        ],
        compiler_params=pltpu.CompilerParams(
            collective_id=0, has_side_effects=True, vmem_limit_bytes=50 * 2**20
        ),
    )(act[0], cotangent[0], expert_ids[0], gate_values[0], w_gate[0], w_up[0], w_down_t[0])
    return tuple(out[None] for out in outs)


def solution(mesh):
    rows = P("section", ("expert", "dp"), None)
    weights = P("section", "dp", "expert")
    return jax.shard_map(
        per_device,
        mesh=mesh,
        in_specs=(rows,) * 4 + (weights,) * 3,
        out_specs=(rows,) * 2 + (weights,) * 3,
        check_vma=False,
    )
```

time: 304 us -> 171 us (0.56)
  waiting for transfers between devices: 203 us -> 0 us
  Pallas kernels: 0 us -> 159 us
  starting transfers between devices: 34.9 us -> 0 us
  matrix products: 20.3 us -> 0 us
  other arithmetic: 14.9 us -> 0 us
  between operations: 14.3 us -> 0.66 us
  local copies, waits for them, and re-layouts: 16.3 us -> 8.19 us
    pallas_call x0 -> x1, Pallas kernels: none -> 159 us  [per_device(): pl.pallas_call(kernel, name='moe_relay', out_shape=[jax.ShapeDtypeStruct(...]
    all_to_all x4 -> x0, waiting for transfers between devices: 136 us -> none  [the longest x1 40.5 us: per_device(): lax.all_to_all(d_send, 'expert', split_axis=0, concat_axis=0, tiled=True)]
    ppermute x2 -> x0, waiting for transfers between devices: 48.2 us -> none  [passed_along(): return lax.ppermute(block, axis, route)]
    all_to_all x4 -> x0, starting transfers between devices: 25.1 us -> none  [the longest x1 10.6 us: per_device(): lax.all_to_all(x_send, 'expert', split_axis=0, concat_axis=0, tiled=True)]
    dot_general x13 -> x0, matrix products: 20.3 us -> none  [the longest x3 5.68 us: right_dot(): lax.dot_general(left, right, (((1,), (1,)), ((), ())), preferred_element_...]
    all_gather x1 -> x0, waiting for transfers between devices: 18.4 us -> none  [per_device(): gathered = lax.all_gather(stacked, 'dp', axis=1, tiled=True)]
    ppermute x2 -> x0, starting transfers between devices: 9.59 us -> none  [passed_along(): return lax.ppermute(block, axis, route)]
    gather x4 -> x0, local copies, waits for them, and re-layouts: 8.65 us -> none  [the longest x2 4.9 us: per_device(): jnp.take(y_total[expert], picked, axis=0)]
  transfers between devices with their start and end apart: 8 -> 0, of which waited for: 7 -> 0; matrix products, arithmetic and copies ran while one was open for 12% -> 0% of each run, Pallas kernels for 0% -> 0%
where the time goes in v1:
time: 171 us; the launch traced here: 168 us
  Pallas kernels  159 us (93%)
  local copies, waits for them, and re-layouts  8.19 us (5%)
    pallas_call x1, Pallas kernels, per_device(): pl.pallas_call(kernel, name='moe_relay', out_shape=[jax.ShapeDtypeStruct(...  159 us
    unnamed x17, local copies, waits for them, and re-layouts  8.19 us

profile of v1, /device:TPU:6, one launch (start us, length us, event | category | flops | bytes accessed | tf_op | source)
XLA Modules:
  0.0 168.0 jit_solution(4006695042769002768)
XLA Ops:
  0.6 0.0 copy-start.3
  0.6 0.7 copy-done.3
  1.3 0.0 copy-start.4
  1.3 0.1 copy.12
  1.4 0.6 copy-done.4
  2.0 0.1 copy.13
  2.1 0.0 copy-start
  2.1 0.9 copy-done
  3.0 0.0 copy-start.1
  3.0 0.9 copy-done.1
  4.0 0.0 copy-start.2
  4.0 0.9 copy-done.2
  4.9 159.2 %moe_relay.1 = (bf16[128,3584]{1,0:T(8,128)(2,1)S(1)}, bf16[128,3584]{1,0:T(8,128)(2,1)S(1)}, bf16[896,128]{1,0:T(8,128)(2,1)S(1)}, bf16[896,128]{1,0:T(8,128)(2,1)S(1)}, bf16[896,128]{1,0:T(8,128)(2,1)S(1)}) custom-call(bf16[128,3584]{1,0:T(8,128)(2,1)} %bitcast.22, bf16[128,3584]{1,0:T(8,128)(2,1)} %bitcast.23, s32[128,8]{1,0:T(8,128)S(1)} %bitcast.14, ...), custom_call_target="tpu_custom_call" | custom-call | tf_op jit(solution)/shard_map/moe_relay/pallas_call | solution.py:310
  164.1 0.9 copy.19
  165.0 0.9 copy.20
  165.9 0.7 copy.21
  166.6 0.7 copy.22
  167.3 0.7 copy.23
Async XLA Ops:
  0.6 0.7 copy-start.3
  1.3 0.7 copy-start.4
  2.1 0.9 copy-start
  3.0 0.9 copy-start.1
  4.0 0.9 copy-start.2

commit v2 on v1

v2 whole, which is shorter than its diff:
```python
import jax
import jax.numpy as jnp
from jax import lax
from jax.experimental import pallas as pl
from jax.experimental.pallas import tpu as pltpu
from jax.sharding import PartitionSpec as P

MESH = pl.DeviceIdType.MESH
EXPERTS = 2
CAP = 16
F32 = jnp.float32
BF16 = jnp.bfloat16


def dot(left, right, left_dim, right_dim, precision=None):
    return lax.dot_general(
        left,
        right,
        (((left_dim,), (right_dim,)), ((), ())),
        preferred_element_type=F32,
        precision=precision,
    )


def kernel(
    act_h, cot_h, ids_h, gates_h, w_gate, w_up, w_down,
    next_act, prev_grad, d_gate_out, d_up_out, d_down_out,
    act, cot, ids, gates,
    wf, pk, rb, xg, picks, pick_prev, pick_next, act_in, cot_in, via_in, via_out,
    normed, hp, hf, hr, ag, yp, rs, fin, ysend, dsend, yin, din, dw_mine, dw_send, dw_in,
    l_s, w_s, w_r, a_s, a_r, sh_s, sh_r, bi_s, bo_s, b_r, p_s, p_r, g_s, g_r,
    di_s, do_s, d_r, e_s, e_r, x_s, x_r, q_s, q_r,
):
    sec, ex, d = lax.axis_index("section"), lax.axis_index("expert"), lax.axis_index("dp")
    z, c = ex // 2, ex % 2
    q, half = z % 4, z // 4
    sx, sy = sec % 4, sec // 4
    sgn = 1 - 2 * (q // 2)
    qm = q * (1 - q // 2) + (3 - q) * (q // 2)
    edge = 1 - qm
    is_edge, is_inner = qm == 0, qm == 1
    width = act.shape[1]
    chunk = width // 4
    cols = w_gate.shape[1]

    def z_dev(step):
        return {"expert": lax.rem(z + step + 8, 8) * 2 + c}

    inward, outward, beyond = z_dev(sgn), z_dev(-sgn), z_dev(-2 * sgn)
    sibling = {"expert": z * 2 + 1 - c}
    dp_dev = [{"dp": lax.rem(d + r + 1, 4)} for r in range(3)]
    sec_next = {"section": lax.rem(sec + 1, 8)}
    sec_prev = {"section": lax.rem(sec + 7, 8)}
    sec_skip = {"section": sy * 4 + lax.rem(sx + 2, 4)}
    sec_over = {"section": lax.rem(sec + 4, 8)}

    def fetch(src, dst, k):
        copy = pltpu.make_async_copy(src, dst, l_s.at[k])
        copy.start()
        return copy

    small = [fetch(ids_h, ids, 0), fetch(gates_h, gates, 1)]
    big = [fetch(act_h, act, 2), fetch(cot_h, cot, 3)]
    weights = []
    for k, w in enumerate((w_gate, w_up, w_down)):
        at = pl.ds(pl.multiple_of(2 * cols * k + c * cols, cols), cols)
        weights.append(fetch(w, wf.at[:, at], 4 + k))

    bar = pltpu.get_barrier_semaphore()
    partners = (inward, outward, beyond, sibling, *dp_dev, sec_next, sec_prev, sec_skip, sec_over)
    for dev in partners:
        pl.semaphore_signal(bar, inc=1, device_id=dev, device_id_type=MESH)

    for copy in small:
        copy.wait()
    tokens = act.shape[0]
    upper = (
        lax.broadcasted_iota(jnp.int32, (tokens, tokens), 0)
        <= lax.broadcasted_iota(jnp.int32, (tokens, tokens), 1)
    ).astype(BF16)
    slots = lax.broadcasted_iota(jnp.int32, (CAP, tokens), 0).astype(F32)
    slot_gate = []
    for e in range(EXPERTS):
        named = jnp.where(ids[...] == e, 1.0, 0.0)
        gate_of = jnp.sum(named * gates[...], axis=0, keepdims=True)
        routed = jnp.sum(named, axis=0, keepdims=True)
        within = dot(jnp.broadcast_to(routed, (8, tokens)).astype(BF16), upper, 1, 0)[0:1] - 1.0
        pick = jnp.where((slots == within) & (routed > 0.5), 1.0, 0.0)
        slot_gate.append(jnp.sum(pick * gate_of, axis=1, keepdims=True))
        picks[e * CAP : (e + 1) * CAP] = pick.astype(BF16)
    slot_gates = jnp.concatenate(slot_gate, axis=0)
    for copy in big:
        copy.wait()
    x_rows = dot(picks[...], act[...], 1, 0)
    inv_root = lax.rsqrt(jnp.mean(x_rows * x_rows, axis=1, keepdims=True) + 1e-6)
    x_rows = x_rows * inv_root
    normed[...] = x_rows
    x_rows = x_rows.astype(BF16)
    g_rows = (slot_gates * dot(picks[...], cot[...], 1, 0)).astype(BF16)
    for e in range(EXPERTS):
        pk[e, 0] = x_rows[e * CAP : (e + 1) * CAP]
        pk[e, 1] = g_rows[e * CAP : (e + 1) * CAP]
    for copy in weights:
        copy.wait()

    pl.semaphore_wait(bar, len(partners))

    pending = []

    def make(src, dst, s, r, dev):
        return pltpu.make_async_remote_copy(
            src_ref=src, dst_ref=dst, send_sem=s, recv_sem=r, device_id=dev, device_id_type=MESH
        )

    def send(src, dst, s, r, dev, pred=None):
        def build():
            return make(src, dst, s, r, dev)

        if pred is None:
            build().start()
        else:
            pl.when(pred)(lambda: build().start())
        pending.append((pred, build))

    def arrived(dst, r, s, dev):
        make(dst, dst, s, r, dev).wait_recv()

    at_edge, at_inner = (0, -2, -1, 1, 2, 3, 5, 4), (0, 1, -1, 2, -3, -2, 4, 3)
    group = [lax.rem(z + sgn * (i + edge * (o - i)) + 16, 8) for o, i in zip(at_edge, at_inner)]

    for r in range(3):
        there = lax.rem(d + r + 1, 4)
        at = pl.ds(pl.multiple_of(there * chunk, 128), chunk)
        send(pk.at[:, :, :, at], rb.at[:, :, d], a_s.at[r], a_r.at[r], dp_dev[r])
    own_at = pl.ds(pl.multiple_of(d * chunk, 128), chunk)
    for e in range(EXPERTS):
        for t in range(2):
            rb[e, t, d] = pk[e, t, :, own_at]
    for k, w in enumerate((w_gate, w_up, w_down)):
        at = pl.ds(pl.multiple_of(2 * cols * k + c * cols, cols), cols)
        send(w, wf.at[:, at], w_s.at[k], w_r.at[k], sibling)
    for r in range(3):
        arrived(rb.at[:, :, lax.rem(d + 3 - r, 4)], a_r.at[r], a_s.at[r], dp_dev[r])

    reach = z_dev(-sgn * (1 + qm))
    for t in range(2):
        send(rb.at[1 - half, t], xg.at[z, t], bo_s.at[8, t], b_r.at[z, t], reach)
        send(rb.at[half, t], xg.at[z, t], bi_s.at[0, t], b_r.at[z, t], inward)
    for t in range(2):
        send(rb.at[half, t], xg.at[z, t], bo_s.at[0, t], b_r.at[z, t], outward, is_inner)

    mid = tokens // 2
    low, high = pl.ds(0, mid), pl.ds(mid, mid)
    send(picks, pick_prev, sh_s.at[4], sh_r.at[4], sec_next)
    send(picks, pick_next, sh_s.at[5], sh_r.at[5], sec_prev)
    send(act.at[high], via_in, sh_s.at[1], sh_r.at[6], sec_skip, sx == 3)
    send(cot.at[high], via_in, sh_s.at[3], sh_r.at[6], sec_skip, sx == 0)
    for k, rows in ((0, low), (1, high)):
        send(act.at[rows], act_in.at[rows], sh_s.at[k], sh_r.at[k], sec_next, sx != 3)
        send(cot.at[rows], cot_in.at[rows], sh_s.at[2 + k], sh_r.at[2 + k], sec_prev, sx != 0)
    is_via = (sx == 1) | (sx == 2)

    xg[z] = rb[half]
    for k in range(3):
        at = pl.ds(pl.multiple_of(2 * cols * k + (1 - c) * cols, cols), cols)
        arrived(wf.at[:, at], w_r.at[k], w_s.at[k], sibling)

    hidden = 2 * cols
    rows = 4 * CAP

    def front(j):
        g = group[j]
        for t in range(2):
            if j > 0:
                arrived(xg.at[g, t], b_r.at[g, t], bo_s.at[0, t], inward)
            if j in (1, 2):
                send(xg.at[g, t], xg.at[g, t], bi_s.at[j, t], b_r.at[g, t], inward, is_edge)
            if j in (1, 3, 6, 7):
                send(xg.at[g, t], xg.at[g, t], bo_s.at[j, t], b_r.at[g, t], outward, is_inner)
            if j in (2, 4, 5):
                send(xg.at[g, t], xg.at[g, t], bi_s.at[j, t], b_r.at[g, t], inward, is_inner)
        x = xg[g, 0].reshape(rows, chunk)
        gr = xg[g, 1].reshape(rows, chunk)
        part = jnp.concatenate(
            [dot(x, wf[:, : 2 * hidden], 1, 0), dot(gr, wf[:, 2 * hidden :], 1, 0)], axis=1
        ).reshape(4, CAP, 3 * hidden)
        hf[j] = part
        hp[j] = part.astype(BF16)
        for r in range(3):
            there = lax.rem(d + r + 1, 4)
            send(hp.at[j, there], hr.at[j, r], p_s.at[j, r], p_r.at[j, r], dp_dev[r])

    def middle(j):
        g = group[j]
        total = hf[j, d]
        for r in range(3):
            arrived(hr.at[j, r], p_r.at[j, r], p_s.at[j, r], dp_dev[r])
            total = total + hr[j, r].astype(F32)
        pre_gate = total[:, :hidden]
        pre_up = total[:, hidden : 2 * hidden]
        hidden_grad = total[:, 2 * hidden :]
        sig = jax.nn.sigmoid(pre_gate)
        silu = pre_gate * sig
        ag[g, d, :, :hidden] = (hidden_grad * pre_up * sig * (1.0 + pre_gate * (1.0 - sig))).astype(BF16)
        ag[g, d, :, hidden : 2 * hidden] = (hidden_grad * silu).astype(BF16)
        ag[g, d, :, 2 * hidden :] = (silu * pre_up).astype(BF16)
        for r in range(3):
            send(ag.at[g, d], ag.at[g, d], g_s.at[j, r], g_r.at[j, r], dp_dev[r])

    def back(j):
        g = group[j]
        for r in range(3):
            arrived(ag.at[g, lax.rem(d + 3 - r, 4)], g_r.at[j, r], g_s.at[j, r], dp_dev[r])
        h = ag[g].reshape(rows, 3 * hidden)
        slot = 8 if j == 3 else g
        for t, (a, b) in enumerate(((2 * hidden, 3 * hidden), (0, 2 * hidden))):
            yp[g, t] = dot(h[:, a:b], wf[:, a:b], 1, 1).astype(BF16).reshape(4, CAP, chunk)
            if j >= 3:
                send(yp.at[g, t], rs.at[slot, t], di_s.at[j, t], d_r.at[slot, t], inward, is_edge)

    def add(g, t, slot):
        yp[g, t] = (yp[g, t].astype(F32) + rs[slot, t].astype(F32)).astype(BF16)

    def chain(j, pred, s, dev, slot=None):
        g = group[j]
        slot = g if slot is None else slot
        for t in range(2):

            @pl.when(pred)
            def _():
                arrived(rs.at[g, t], d_r.at[g, t], do_s.at[0, t], inward)
                add(g, t, g)

            send(yp.at[g, t], rs.at[slot, t], s.at[j, t], d_r.at[slot, t], dev, pred)

    def home(src, e, k, pred=None):
        for r in range(3):
            there = lax.rem(d + r + 1, 4)
            send(src.at[:, there], fin.at[e, :, :, own_at], e_s.at[k, r], e_r.at[k, r], dp_dev[r], pred)

        def own():
            fin[e, :, :, own_at] = src[:, d]

        if pred is None:
            own()
        else:
            pl.when(pred)(own)

    def finish(pred, both):
        @pl.when(pred)
        def _():
            for t in range(2):
                arrived(rs.at[z, t], d_r.at[z, t], do_s.at[0, t], inward)
                add(z, t, z)
                if both:
                    arrived(rs.at[8, t], d_r.at[8, t], do_s.at[0, t], outward)
                    add(z, t, 8)

        home(yp.at[z], half, 0, pred)

    for j in range(8):
        front(j)
        if j >= 1:
            middle(j - 1)
        if j >= 2:
            back(j - 2)
    chain(1, is_inner, di_s, inward)
    finish(is_inner, True)
    middle(7)

    send(act.at[low], act_in.at[low], sh_s.at[0], sh_r.at[0], sec_next, sx == 3)
    send(cot.at[low], cot_in.at[low], sh_s.at[2], sh_r.at[2], sec_prev, sx == 0)

    @pl.when(is_via)
    def _():
        arrived(via_in, sh_r.at[6], sh_s.at[6], sec_skip)

    send(via_in, via_out, sh_s.at[6], sh_r.at[7], sec_over, is_via)

    back(6)
    chain(3, is_inner, di_s, inward)
    chain(2, is_inner, do_s, outward)
    back(7)
    chain(6, is_inner, di_s, inward)
    chain(4, is_inner, do_s, outward)
    finish(is_edge, False)
    chain(1, is_edge, do_s, beyond, 9)
    chain(7, is_inner, di_s, inward)
    chain(5, is_inner, do_s, outward)
    chain(2, is_edge, do_s, outward, 9)

    h_all = ag[...].reshape(8 * rows, 3 * hidden)
    x_all = xg[:, 0].reshape(8 * rows, chunk)
    dw_mine[:, : 2 * hidden] = dot(x_all, h_all[:, : 2 * hidden], 0, 0)
    g_all = xg[:, 1].reshape(8 * rows, chunk)
    dw_mine[:, 2 * hidden :] = dot(g_all, h_all[:, 2 * hidden :], 0, 0)
    for k in range(3):
        at = pl.ds(pl.multiple_of(hidden * k + (1 - c) * cols, cols), cols)
        dw_send[k] = dw_mine[:, at].astype(BF16)
        send(dw_send.at[k], dw_in.at[k], q_s.at[k], q_r.at[k], sibling)

    def leave(e, k):
        for r in range(3):
            there = lax.rem(d + 3 - r, 4)
            at = pl.ds(pl.multiple_of(there * chunk, 128), chunk)
            arrived(fin.at[e, :, :, at], e_r.at[k, r], e_s.at[k, r], dp_dev[r])
        at = pl.ds(pl.multiple_of(e * CAP, CAP), CAP)
        pick_half = e == 0
        gate = jnp.where(pick_half, slot_gates[:CAP], slot_gates[CAP:])
        root = jnp.where(pick_half, inv_root[:CAP], inv_root[CAP:])
        ysend[at] = (gate * fin[e, 0].astype(F32)).astype(BF16)
        send(ysend.at[at], yin.at[at], x_s.at[0, k], x_r.at[0, k], sec_next)
        d_rows = fin[e, 1].astype(F32)
        n_rows = normed[at]
        spread = jnp.mean(n_rows * d_rows, axis=1, keepdims=True)
        dsend[at] = (root * (d_rows - n_rows * spread)).astype(BF16)
        send(dsend.at[at], din.at[at], x_s.at[1, k], x_r.at[1, k], sec_prev)

    leave(half, 0)

    @pl.when(is_via)
    def _():
        arrived(via_out, sh_r.at[7], sh_s.at[7], sec_over)

    send(via_out, act_in.at[high], sh_s.at[7], sh_r.at[1], sec_prev, sx == 1)
    send(via_out, cot_in.at[high], sh_s.at[7], sh_r.at[3], sec_next, sx == 2)

    for t in range(2):
        arrived(rs.at[9, t], d_r.at[9, t], do_s.at[0, t], outward)
    home(rs.at[9], 1 - half, 1)
    leave(1 - half, 1)

    for k, out in enumerate((d_gate_out, d_up_out, d_down_out)):
        arrived(dw_in.at[k], q_r.at[k], q_s.at[k], sibling)
        at = pl.ds(pl.multiple_of(hidden * k + c * cols, cols), cols)
        out[...] = (dw_mine[:, at] + dw_in[k].astype(F32)).astype(BF16)

    for t, (out, kept, pick, extra, dev) in enumerate(
        ((next_act, act_in, pick_prev, yin, sec_next), (prev_grad, cot_in, pick_next, din, sec_prev))
    ):
        arrived(pick, sh_r.at[4 + t], sh_s.at[4 + t], dev)
        arrived(kept.at[low], sh_r.at[2 * t], sh_s.at[2 * t], dev)
        arrived(kept.at[high], sh_r.at[2 * t + 1], sh_s.at[2 * t + 1], dev)
        for k, e in ((0, half), (1, 1 - half)):
            at = pl.ds(pl.multiple_of(e * CAP, CAP), CAP)
            arrived(extra.at[at], x_r.at[t, k], x_s.at[t, k], dev)
        out[...] = (kept[...].astype(F32) + dot(pick[...], extra[...], 0, 0)).astype(BF16)

    for pred, build in pending:
        if pred is None:
            build().wait_send()
        else:
            pl.when(pred)(lambda build=build: build().wait_send())


def per_device(act, cotangent, expert_ids, gate_values, w_gate, w_up, w_down_t):
    tokens, width = act.shape[1:]
    depth, cols = w_gate.shape[1:]
    chunk, hidden = width // 4, 2 * cols
    vmem = pl.BlockSpec(memory_space=pltpu.VMEM)
    anywhere = pl.BlockSpec(memory_space=pltpu.HBM)
    dma = pltpu.SemaphoreType.DMA
    slots = EXPERTS * CAP
    topk = expert_ids.shape[2]
    outs = pl.pallas_call(
        kernel,
        name="moe_relay",
        out_shape=[
            jax.ShapeDtypeStruct((tokens, width), BF16),
            jax.ShapeDtypeStruct((tokens, width), BF16),
            jax.ShapeDtypeStruct((depth, cols), BF16),
            jax.ShapeDtypeStruct((depth, cols), BF16),
            jax.ShapeDtypeStruct((depth, cols), BF16),
        ],
        in_specs=[anywhere] * 7,
        out_specs=[vmem] * 5,
        scratch_shapes=[
            pltpu.VMEM((tokens, width), BF16),
            pltpu.VMEM((tokens, width), BF16),
            pltpu.VMEM((topk, tokens), jnp.int32),
            pltpu.VMEM((topk, tokens), F32),
            pltpu.VMEM((depth, 3 * hidden), BF16),
            pltpu.VMEM((EXPERTS, 2, CAP, width), BF16),
            pltpu.VMEM((EXPERTS, 2, 4, CAP, chunk), BF16),
            pltpu.VMEM((8, 2, 4, CAP, chunk), BF16),
            pltpu.VMEM((slots, tokens), BF16),
            pltpu.VMEM((slots, tokens), BF16),
            pltpu.VMEM((slots, tokens), BF16),
            pltpu.VMEM((tokens, width), BF16),
            pltpu.VMEM((tokens, width), BF16),
            pltpu.VMEM((tokens // 2, width), BF16),
            pltpu.VMEM((tokens // 2, width), BF16),
            pltpu.VMEM((slots, width), F32),
            pltpu.VMEM((8, 4, CAP, 3 * hidden), BF16),
            pltpu.VMEM((8, 4, CAP, 3 * hidden), F32),
            pltpu.VMEM((8, 3, CAP, 3 * hidden), BF16),
            pltpu.VMEM((8, 4, CAP, 3 * hidden), BF16),
            pltpu.VMEM((8, 2, 4, CAP, chunk), BF16),
            pltpu.VMEM((10, 2, 4, CAP, chunk), BF16),
            pltpu.VMEM((EXPERTS, 2, CAP, width), BF16),
            pltpu.VMEM((slots, width), BF16),
            pltpu.VMEM((slots, width), BF16),
            pltpu.VMEM((slots, width), BF16),
            pltpu.VMEM((slots, width), BF16),
            pltpu.VMEM((depth, 3 * hidden), F32),
            pltpu.VMEM((3, depth, cols), BF16),
            pltpu.VMEM((3, depth, cols), BF16),
            dma((7,)),
            dma((3,)), dma((3,)),
            dma((3,)), dma((3,)),
            dma((8,)), dma((8,)),
            dma((8, 2)), dma((9, 2)), dma((8, 2)),
            dma((8, 3)), dma((8, 3)),
            dma((8, 3)), dma((8, 3)),
            dma((8, 2)), dma((8, 2)), dma((10, 2)),
            dma((2, 3)), dma((2, 3)),
            dma((2, 2)), dma((2, 2)),
            dma((3,)), dma((3,)),
        ],
        compiler_params=pltpu.CompilerParams(
            collective_id=0, has_side_effects=True, vmem_limit_bytes=50 * 2**20
        ),
    )(
        act[0],
        cotangent[0],
        jnp.swapaxes(expert_ids[0], 0, 1),
        jnp.swapaxes(gate_values[0], 0, 1),
        w_gate[0],
        w_up[0],
        w_down_t[0],
    )
    return tuple(out[None] for out in outs)


def solution(mesh):
    rows = P("section", ("expert", "dp"), None)
    weights = P("section", "dp", "expert")
    return jax.shard_map(
        per_device,
        mesh=mesh,
        in_specs=(rows,) * 4 + (weights,) * 3,
        out_specs=(rows,) * 2 + (weights,) * 3,
        check_vma=False,
    )
```

time: 171 us -> 141 us (0.82)
  the two profiles are of different devices: /device:TPU:6 before, /device:TPU:24 now
where the time goes in v2:
time: 141 us
  Pallas kernels  133 us (94%)
  local copies, waits for them, and re-layouts  7.41 us (5%)
    pallas_call x1, Pallas kernels, per_device(): pl.pallas_call(kernel, name='moe_relay', out_shape=[jax.ShapeDtypeStruct(...  133 us
    unnamed x15, local copies, waits for them, and re-layouts  7.41 us

profile of v2, /device:TPU:24, one launch (start us, length us, event | category | flops | bytes accessed | tf_op | source)
XLA Modules:
  0.0 141.2 jit_solution(8259886551062632638)
XLA Ops:
  0.6 0.0 copy-start.4
  0.6 0.0 copy-start.3
  0.7 0.7 copy-done.4
  1.3 0.0 copy-done.3
  1.3 0.0 copy-start
  1.3 0.9 copy-done
  2.3 0.0 copy-start.1
  2.3 0.9 copy-done.1
  3.2 0.0 copy-start.2
  3.2 0.9 copy-done.2
  4.2 133.1 %moe_relay.1 = (bf16[128,3584]{1,0:T(8,128)(2,1)S(1)}, bf16[128,3584]{1,0:T(8,128)(2,1)S(1)}, bf16[896,128]{1,0:T(8,128)(2,1)S(1)}, bf16[896,128]{1,0:T(8,128)(2,1)S(1)}, bf16[896,128]{1,0:T(8,128)(2,1)S(1)}) custom-call(bf16[128,3584]{1,0:T(8,128)(2,1)} %bitcast.26, bf16[128,3584]{1,0:T(8,128)(2,1)} %bitcast.27, s32[8,128]{1,0:T(8,128)S(1)} %bitcast.24, ...), custom_call_target="tpu_custom_call" | custom-call | tf_op jit(solution)/shard_map/moe_relay/pallas_call | solution.py:365
  137.3 0.9 copy.17
  138.2 0.9 copy.18
  139.1 0.7 copy.19
  139.8 0.7 copy.20
  140.5 0.7 copy.21
Async XLA Ops:
  0.6 0.7 copy-start.4
  0.6 0.7 copy-start.3
  1.3 0.9 copy-start
  2.3 0.9 copy-start.1
  3.2 0.9 copy-start.2

commit v3 on v2

--- a/solution.py
+++ b/solution.py
@@ -8,6 +8,7 @@
 MESH = pl.DeviceIdType.MESH
 EXPERTS = 2
 CAP = 16
+VIA = 5
 F32 = jnp.float32
 BF16 = jnp.bfloat16
 
@@ -27,8 +28,8 @@
     next_act, prev_grad, d_gate_out, d_up_out, d_down_out,
     act, cot, ids, gates,
     wf, pk, rb, xg, picks, pick_prev, pick_next, act_in, cot_in, via_in, via_out,
-    normed, hp, hf, hr, ag, yp, rs, fin, ysend, dsend, yin, din, dw_mine, dw_send, dw_in,
-    l_s, w_s, w_r, a_s, a_r, sh_s, sh_r, bi_s, bo_s, b_r, p_s, p_r, g_s, g_r,
+    normed, hp, hf, hr, hs, ht, ag, yp, rs, fin, ysend, dsend, yin, din, dw_mine, dw_send, dw_in,
+    l_s, w_s, w_r, a_s, a_r, sh_s, sh_r, v_s, v_r, bi_s, bo_s, b_r, p_s, p_r, g_s, g_r,
     di_s, do_s, d_r, e_s, e_r, x_s, x_r, q_s, q_r,
 ):
     sec, ex, d = lax.axis_index("section"), lax.axis_index("expert"), lax.axis_index("dp")
@@ -48,6 +49,8 @@
 
     inward, outward, beyond = z_dev(sgn), z_dev(-sgn), z_dev(-2 * sgn)
     sibling = {"expert": z * 2 + 1 - c}
+    lo, hi = d % 2, d // 2
+    dp_near, dp_far = {"dp": d + 1 - 2 * lo}, {"dp": lax.rem(d + 2, 4)}
     dp_dev = [{"dp": lax.rem(d + r + 1, 4)} for r in range(3)]
     sec_next = {"section": lax.rem(sec + 1, 8)}
     sec_prev = {"section": lax.rem(sec + 7, 8)}
@@ -128,36 +131,47 @@
     at_edge, at_inner = (0, -2, -1, 1, 2, 3, 5, 4), (0, 1, -1, 2, -3, -2, 4, 3)
     group = [lax.rem(z + sgn * (i + edge * (o - i)) + 16, 8) for o, i in zip(at_edge, at_inner)]
 
-    for r in range(3):
-        there = lax.rem(d + r + 1, 4)
+    both = ((hi, 1 - lo), (1 - hi, lo), (1 - hi, 1 - lo))
+    for r, (pair_of, place) in enumerate(both):
+        there = 2 * pair_of + place
         at = pl.ds(pl.multiple_of(there * chunk, 128), chunk)
-        send(pk.at[:, :, :, at], rb.at[:, :, d], a_s.at[r], a_r.at[r], dp_dev[r])
+        send(pk.at[:, :, :, at], rb.at[:, hi, :, lo], a_s.at[r], a_r.at[r], {"dp": there})
     own_at = pl.ds(pl.multiple_of(d * chunk, 128), chunk)
     for e in range(EXPERTS):
         for t in range(2):
-            rb[e, t, d] = pk[e, t, :, own_at]
+            rb[e, hi, t, lo] = pk[e, t, :, own_at]
     for k, w in enumerate((w_gate, w_up, w_down)):
         at = pl.ds(pl.multiple_of(2 * cols * k + c * cols, cols), cols)
         send(w, wf.at[:, at], w_s.at[k], w_r.at[k], sibling)
-    for r in range(3):
-        arrived(rb.at[:, :, lax.rem(d + 3 - r, 4)], a_r.at[r], a_s.at[r], dp_dev[r])
 
     reach = z_dev(-sgn * (1 + qm))
-    for t in range(2):
-        send(rb.at[1 - half, t], xg.at[z, t], bo_s.at[8, t], b_r.at[z, t], reach)
-        send(rb.at[half, t], xg.at[z, t], bi_s.at[0, t], b_r.at[z, t], inward)
-    for t in range(2):
-        send(rb.at[half, t], xg.at[z, t], bo_s.at[0, t], b_r.at[z, t], outward, is_inner)
-
-    mid = tokens // 2
-    low, high = pl.ds(0, mid), pl.ds(mid, mid)
+
+    def set_out(p):
+        pair_of = hi if p == 0 else 1 - hi
+        send(rb.at[1 - half, pair_of], xg.at[z, pair_of], bo_s.at[8, p], b_r.at[z, p], reach)
+        send(rb.at[half, pair_of], xg.at[z, pair_of], bi_s.at[0, p], b_r.at[z, p], inward)
+        send(rb.at[half, pair_of], xg.at[z, pair_of], bo_s.at[0, p], b_r.at[z, p], outward, is_inner)
+
+    arrived(rb.at[:, hi, :, 1 - lo], a_r.at[0], a_s.at[0], dp_near)
+    set_out(0)
+    for r in (1, 2):
+        pair_of, place = both[r]
+        arrived(rb.at[:, pair_of, :, place], a_r.at[r], a_s.at[r], {"dp": 2 * pair_of + place})
+    set_out(1)
+
+    piece = CAP
+    mid = tokens - VIA * piece
+    low, high = pl.ds(0, mid), pl.ds(mid, VIA * piece)
+    parts = [pl.ds(mid + k * piece, piece) for k in range(VIA)]
     send(picks, pick_prev, sh_s.at[4], sh_r.at[4], sec_next)
     send(picks, pick_next, sh_s.at[5], sh_r.at[5], sec_prev)
     send(act.at[high], via_in, sh_s.at[1], sh_r.at[6], sec_skip, sx == 3)
     send(cot.at[high], via_in, sh_s.at[3], sh_r.at[6], sec_skip, sx == 0)
-    for k, rows in ((0, low), (1, high)):
-        send(act.at[rows], act_in.at[rows], sh_s.at[k], sh_r.at[k], sec_next, sx != 3)
-        send(cot.at[rows], cot_in.at[rows], sh_s.at[2 + k], sh_r.at[2 + k], sec_prev, sx != 0)
+    send(act.at[low], act_in.at[low], sh_s.at[0], sh_r.at[0], sec_next, sx != 3)
+    send(cot.at[low], cot_in.at[low], sh_s.at[2], sh_r.at[2], sec_prev, sx != 0)
+    for k, part in enumerate(parts):
+        send(act.at[part], act_in.at[part], v_s.at[0, k], v_r.at[0, k], sec_next, sx != 3)
+        send(cot.at[part], cot_in.at[part], v_s.at[1, k], v_r.at[1, k], sec_prev, sx != 0)
     is_via = (sx == 1) | (sx == 2)
 
     xg[z] = rb[half]
@@ -168,55 +182,85 @@
     hidden = 2 * cols
     rows = 4 * CAP
 
+    def receive(j, p):
+        g = group[j]
+        pair_of = hi if p == 0 else 1 - hi
+        piece_of = xg.at[g, pair_of]
+        if j > 0:
+            arrived(piece_of, b_r.at[g, p], bo_s.at[0, p], inward)
+        if j in (1, 2):
+            send(piece_of, piece_of, bi_s.at[j, p], b_r.at[g, p], inward, is_edge)
+        if j in (1, 3, 6, 7):
+            send(piece_of, piece_of, bo_s.at[j, p], b_r.at[g, p], outward, is_inner)
+        if j in (2, 4, 5):
+            send(piece_of, piece_of, bi_s.at[j, p], b_r.at[g, p], inward, is_inner)
+
     def front(j):
         g = group[j]
-        for t in range(2):
-            if j > 0:
-                arrived(xg.at[g, t], b_r.at[g, t], bo_s.at[0, t], inward)
-            if j in (1, 2):
-                send(xg.at[g, t], xg.at[g, t], bi_s.at[j, t], b_r.at[g, t], inward, is_edge)
-            if j in (1, 3, 6, 7):
-                send(xg.at[g, t], xg.at[g, t], bo_s.at[j, t], b_r.at[g, t], outward, is_inner)
-            if j in (2, 4, 5):
-                send(xg.at[g, t], xg.at[g, t], bi_s.at[j, t], b_r.at[g, t], inward, is_inner)
-        x = xg[g, 0].reshape(rows, chunk)
-        gr = xg[g, 1].reshape(rows, chunk)
-        part = jnp.concatenate(
+        x = xg[g, :, 0].reshape(rows, chunk)
+        gr = xg[g, :, 1].reshape(rows, chunk)
+        hf[j] = jnp.concatenate(
             [dot(x, wf[:, : 2 * hidden], 1, 0), dot(gr, wf[:, 2 * hidden :], 1, 0)], axis=1
-        ).reshape(4, CAP, 3 * hidden)
-        hf[j] = part
-        hp[j] = part.astype(BF16)
-        for r in range(3):
-            there = lax.rem(d + r + 1, 4)
-            send(hp.at[j, there], hr.at[j, r], p_s.at[j, r], p_r.at[j, r], dp_dev[r])
+        ).reshape(2, 2, CAP, 3 * hidden)
+        hp[j] = hf[j, :, 1 - lo].astype(BF16)
+        send(hp.at[j], hr.at[j], p_s.at[j, 0], p_r.at[j, 0], dp_near)
+
+    def pair(j):
+        arrived(hr.at[j], p_r.at[j, 0], p_s.at[j, 0], dp_near)
+        hs[j] = (hf[j, 1 - hi, lo] + hr[j, 1 - hi].astype(F32)).astype(BF16)
+        send(hs.at[j], ht.at[j], p_s.at[j, 1], p_r.at[j, 1], dp_far)
 
     def middle(j):
         g = group[j]
-        total = hf[j, d]
-        for r in range(3):
-            arrived(hr.at[j, r], p_r.at[j, r], p_s.at[j, r], dp_dev[r])
-            total = total + hr[j, r].astype(F32)
+        total = hf[j, hi, lo] + hr[j, hi].astype(F32)
+        arrived(ht.at[j], p_r.at[j, 1], p_s.at[j, 1], dp_far)
+        total = total + ht[j].astype(F32)
         pre_gate = total[:, :hidden]
         pre_up = total[:, hidden : 2 * hidden]
         hidden_grad = total[:, 2 * hidden :]
         sig = jax.nn.sigmoid(pre_gate)
         silu = pre_gate * sig
-        ag[g, d, :, :hidden] = (hidden_grad * pre_up * sig * (1.0 + pre_gate * (1.0 - sig))).astype(BF16)
-        ag[g, d, :, hidden : 2 * hidden] = (hidden_grad * silu).astype(BF16)
-        ag[g, d, :, 2 * hidden :] = (silu * pre_up).astype(BF16)
-        for r in range(3):
-            send(ag.at[g, d], ag.at[g, d], g_s.at[j, r], g_r.at[j, r], dp_dev[r])
+        ag[g, hi, lo, :, :hidden] = (hidden_grad * pre_up * sig * (1.0 + pre_gate * (1.0 - sig))).astype(BF16)
+        ag[g, hi, lo, :, hidden : 2 * hidden] = (hidden_grad * silu).astype(BF16)
+        ag[g, hi, lo, :, 2 * hidden :] = (silu * pre_up).astype(BF16)
+        send(ag.at[g, hi, lo], ag.at[g, hi, lo], g_s.at[j, 0], g_r.at[j, 0], dp_far)
+
+    def spread_out(j):
+        g = group[j]
+        arrived(ag.at[g, 1 - hi, lo], g_r.at[j, 0], g_s.at[j, 0], dp_far)
+        send(ag.at[g, :, lo], ag.at[g, :, lo], g_s.at[j, 1], g_r.at[j, 1], dp_near)
 
     def back(j):
         g = group[j]
-        for r in range(3):
-            arrived(ag.at[g, lax.rem(d + 3 - r, 4)], g_r.at[j, r], g_s.at[j, r], dp_dev[r])
+        arrived(ag.at[g, :, 1 - lo], g_r.at[j, 1], g_s.at[j, 1], dp_near)
         h = ag[g].reshape(rows, 3 * hidden)
         slot = 8 if j == 3 else g
         for t, (a, b) in enumerate(((2 * hidden, 3 * hidden), (0, 2 * hidden))):
             yp[g, t] = dot(h[:, a:b], wf[:, a:b], 1, 1).astype(BF16).reshape(4, CAP, chunk)
             if j >= 3:
                 send(yp.at[g, t], rs.at[slot, t], di_s.at[j, t], d_r.at[slot, t], inward, is_edge)
+
+    def cross():
+        send(act.at[low], act_in.at[low], sh_s.at[0], sh_r.at[0], sec_next, sx == 3)
+        send(cot.at[low], cot_in.at[low], sh_s.at[2], sh_r.at[2], sec_prev, sx == 0)
+
+        @pl.when(is_via)
+        def _():
+            arrived(via_in, sh_r.at[6], sh_s.at[6], sec_skip)
+
+        for k in range(VIA):
+            at = pl.ds(k * piece, piece)
+            send(via_in.at[at], via_out.at[at], v_s.at[2, k], v_r.at[2, k], sec_over, is_via)
+
+    def pass_on(k):
+        at = pl.ds(k * piece, piece)
+
+        @pl.when(is_via)
+        def _():
+            arrived(via_out.at[at], v_r.at[2, k], v_s.at[2, k], sec_over)
+
+        send(via_out.at[at], act_in.at[parts[k]], v_s.at[3, k], v_r.at[0, k], sec_prev, sx == 1)
+        send(via_out.at[at], cot_in.at[parts[k]], v_s.at[3, k], v_r.at[1, k], sec_next, sx == 2)
 
     def add(g, t, slot):
         yp[g, t] = (yp[g, t].astype(F32) + rs[slot, t].astype(F32)).astype(BF16)
@@ -259,29 +303,33 @@
         home(yp.at[z], half, 0, pred)
 
     for j in range(8):
+        receive(j, 0)
+        receive(j, 1)
         front(j)
         if j >= 1:
-            middle(j - 1)
+            pair(j - 1)
         if j >= 2:
-            back(j - 2)
+            middle(j - 2)
+        if j >= 3:
+            spread_out(j - 3)
+        if j >= 4:
+            back(j - 4)
+    pair(7)
+    middle(6)
+    spread_out(5)
+    back(4)
+    middle(7)
+    spread_out(6)
+    back(5)
     chain(1, is_inner, di_s, inward)
+    spread_out(7)
     finish(is_inner, True)
-    middle(7)
-
-    send(act.at[low], act_in.at[low], sh_s.at[0], sh_r.at[0], sec_next, sx == 3)
-    send(cot.at[low], cot_in.at[low], sh_s.at[2], sh_r.at[2], sec_prev, sx == 0)
-
-    @pl.when(is_via)
-    def _():
-        arrived(via_in, sh_r.at[6], sh_s.at[6], sec_skip)
-
-    send(via_in, via_out, sh_s.at[6], sh_r.at[7], sec_over, is_via)
-
     back(6)
     chain(3, is_inner, di_s, inward)
     chain(2, is_inner, do_s, outward)
     back(7)
     chain(6, is_inner, di_s, inward)
+    cross()
     chain(4, is_inner, do_s, outward)
     finish(is_edge, False)
     chain(1, is_edge, do_s, beyond, 9)
@@ -289,10 +337,12 @@
     chain(5, is_inner, do_s, outward)
     chain(2, is_edge, do_s, outward, 9)
 
+    pass_on(0)
+    pass_on(1)
     h_all = ag[...].reshape(8 * rows, 3 * hidden)
-    x_all = xg[:, 0].reshape(8 * rows, chunk)
+    x_all = xg[:, :, 0].reshape(8 * rows, chunk)
     dw_mine[:, : 2 * hidden] = dot(x_all, h_all[:, : 2 * hidden], 0, 0)
-    g_all = xg[:, 1].reshape(8 * rows, chunk)
+    g_all = xg[:, :, 1].reshape(8 * rows, chunk)
     dw_mine[:, 2 * hidden :] = dot(g_all, h_all[:, 2 * hidden :], 0, 0)
     for k in range(3):
         at = pl.ds(pl.multiple_of(hidden * k + (1 - c) * cols, cols), cols)
@@ -316,14 +366,9 @@
         dsend[at] = (root * (d_rows - n_rows * spread)).astype(BF16)
         send(dsend.at[at], din.at[at], x_s.at[1, k], x_r.at[1, k], sec_prev)
 
+    for k in range(2, VIA):
+        pass_on(k)
     leave(half, 0)
-
-    @pl.when(is_via)
-    def _():
-        arrived(via_out, sh_r.at[7], sh_s.at[7], sec_over)
-
-    send(via_out, act_in.at[high], sh_s.at[7], sh_r.at[1], sec_prev, sx == 1)
-    send(via_out, cot_in.at[high], sh_s.at[7], sh_r.at[3], sec_next, sx == 2)
 
     for t in range(2):
         arrived(rs.at[9, t], d_r.at[9, t], do_s.at[0, t], outward)
@@ -340,7 +385,8 @@
     ):
         arrived(pick, sh_r.at[4 + t], sh_s.at[4 + t], dev)
         arrived(kept.at[low], sh_r.at[2 * t], sh_s.at[2 * t], dev)
-        arrived(kept.at[high], sh_r.at[2 * t + 1], sh_s.at[2 * t + 1], dev)
+        for k, part in enumerate(parts):
+            arrived(kept.at[part], v_r.at[t, k], v_s.at[t, k], dev)
         for k, e in ((0, half), (1, 1 - half)):
             at = pl.ds(pl.multiple_of(e * CAP, CAP), CAP)
             arrived(extra.at[at], x_r.at[t, k], x_s.at[t, k], dev)
@@ -381,20 +427,22 @@
             pltpu.VMEM((topk, tokens), F32),
             pltpu.VMEM((depth, 3 * hidden), BF16),
             pltpu.VMEM((EXPERTS, 2, CAP, width), BF16),
-            pltpu.VMEM((EXPERTS, 2, 4, CAP, chunk), BF16),
-            pltpu.VMEM((8, 2, 4, CAP, chunk), BF16),
+            pltpu.VMEM((EXPERTS, 2, 2, 2, CAP, chunk), BF16),
+            pltpu.VMEM((8, 2, 2, 2, CAP, chunk), BF16),
             pltpu.VMEM((slots, tokens), BF16),
             pltpu.VMEM((slots, tokens), BF16),
             pltpu.VMEM((slots, tokens), BF16),
             pltpu.VMEM((tokens, width), BF16),
             pltpu.VMEM((tokens, width), BF16),
-            pltpu.VMEM((tokens // 2, width), BF16),
-            pltpu.VMEM((tokens // 2, width), BF16),
+            pltpu.VMEM((VIA * CAP, width), BF16),
+            pltpu.VMEM((VIA * CAP, width), BF16),
             pltpu.VMEM((slots, width), F32),
-            pltpu.VMEM((8, 4, CAP, 3 * hidden), BF16),
-            pltpu.VMEM((8, 4, CAP, 3 * hidden), F32),
-            pltpu.VMEM((8, 3, CAP, 3 * hidden), BF16),
-            pltpu.VMEM((8, 4, CAP, 3 * hidden), BF16),
+            pltpu.VMEM((8, 2, CAP, 3 * hidden), BF16),
+            pltpu.VMEM((8, 2, 2, CAP, 3 * hidden), F32),
+            pltpu.VMEM((8, 2, CAP, 3 * hidden), BF16),
+            pltpu.VMEM((8, CAP, 3 * hidden), BF16),
+            pltpu.VMEM((8, CAP, 3 * hidden), BF16),
+            pltpu.VMEM((8, 2, 2, CAP, 3 * hidden), BF16),
             pltpu.VMEM((8, 2, 4, CAP, chunk), BF16),
             pltpu.VMEM((10, 2, 4, CAP, chunk), BF16),
             pltpu.VMEM((EXPERTS, 2, CAP, width), BF16),
@@ -408,17 +456,18 @@
             dma((7,)),
             dma((3,)), dma((3,)),
             dma((3,)), dma((3,)),
-            dma((8,)), dma((8,)),
+            dma((7,)), dma((7,)),
+            dma((4, VIA)), dma((3, VIA)),
             dma((8, 2)), dma((9, 2)), dma((8, 2)),
-            dma((8, 3)), dma((8, 3)),
-            dma((8, 3)), dma((8, 3)),
+            dma((8, 2)), dma((8, 2)),
+            dma((8, 2)), dma((8, 2)),
             dma((8, 2)), dma((8, 2)), dma((10, 2)),
             dma((2, 3)), dma((2, 3)),
             dma((2, 2)), dma((2, 2)),
             dma((3,)), dma((3,)),
         ],
         compiler_params=pltpu.CompilerParams(
-            collective_id=0, has_side_effects=True, vmem_limit_bytes=50 * 2**20
+            collective_id=0, has_side_effects=True, vmem_limit_bytes=62 * 2**20
         ),
     )(
         act[0],

time: 141 us -> 124 us (0.88)
  the two profiles are of different devices: /device:TPU:24 before, /device:TPU:6 now
where the time goes in v3:
time: 124 us
  Pallas kernels  117 us (94%)
  local copies, waits for them, and re-layouts  6.15 us (5%)
    pallas_call x1, Pallas kernels, per_device(): pl.pallas_call(kernel, name='moe_relay', out_shape=[jax.ShapeDtypeStruct(...  117 us
    unnamed x13, local copies, waits for them, and re-layouts  6.15 us

profile of v3, /device:TPU:6, one launch (start us, length us, event | category | flops | bytes accessed | tf_op | source)
XLA Modules:
  0.0 123.8 jit_solution(3224571548047982185)
XLA Ops:
  0.6 117.0 %moe_relay.1 = (bf16[128,3584]{1,0:T(8,128)(2,1)}, bf16[128,3584]{1,0:T(8,128)(2,1)}, bf16[896,128]{1,0:T(8,128)(2,1)}, bf16[896,128]{1,0:T(8,128)(2,1)}, bf16[896,128]{1,0:T(8,128)(2,1)}) custom-call(bf16[128,3584]{1,0:T(8,128)(2,1)} %bitcast.18, bf16[128,3584]{1,0:T(8,128)(2,1)} %bitcast.19, s32[8,128]{1,0:T(8,128)} %bitcast.26, f32[8,128]{1,0:T(8,128)} %bitcast.27, ...), custom_call_target="tpu_custom_call" | custom-call | tf_op jit(solution)/shard_map/moe_relay/pallas_call | solution.py:411
  117.6 0.0 copy-start
  117.7 2.2 %copy.17 = bf16[1,128,3584]{2,1,0:T(8,128)(2,1)} copy(bf16[1,128,3584]{2,1,0:T(8,128)(2,1)} %bitcast.17) | data formatting | bytes 1835008
  119.9 0.0 copy-done
  119.9 0.0 copy-start.3
  119.9 0.9 copy.18
  120.8 0.3 copy-done.3
  121.1 0.0 copy-start.2
  121.1 0.7 copy.19
  121.8 0.3 copy-done.2
  122.1 0.0 copy-start.1
  122.1 0.7 copy.20
  122.8 0.3 copy-done.1
  123.1 0.7 copy.21
Async XLA Ops:
  117.6 2.3 %copy-start = (bf16[128,3584]{1,0:T(8,128)(2,1)S(1)}, bf16[128,3584]{1,0:T(8,128)(2,1)}, u32[]{:S(2)}) copy-start(bf16[128,3584]{1,0:T(8,128)(2,1)} %get-tuple-element.11) | copy-start | bytes 2752516
  119.9 1.2 copy-start.3
  121.1 1.0 copy-start.2
  122.1 1.0 copy-start.1

commit v4 on v3

--- a/solution.py
+++ b/solution.py
@@ -321,8 +321,8 @@
     middle(7)
     spread_out(6)
     back(5)
+    spread_out(7)
     chain(1, is_inner, di_s, inward)
-    spread_out(7)
     finish(is_inner, True)
     back(6)
     chain(3, is_inner, di_s, inward)

time: 124 us -> 124 us (level); the launches traced: 124 us -> 122 us
  Pallas kernels: 117 us -> 115 us
    pallas_call x1, Pallas kernels: 117 us -> 115 us  [per_device(): pl.pallas_call(kernel, name='moe_relay', out_shape=[jax.ShapeDtypeStruct(...]
where the time goes in v4:
time: 124 us; the launch traced here: 122 us
  Pallas kernels  115 us (93%)
  local copies, waits for them, and re-layouts  6.15 us (5%)
    pallas_call x1, Pallas kernels, per_device(): pl.pallas_call(kernel, name='moe_relay', out_shape=[jax.ShapeDtypeStruct(...  115 us
    unnamed x13, local copies, waits for them, and re-layouts  6.15 us

profile of v4, /device:TPU:6, one launch (start us, length us, event | category | flops | bytes accessed | tf_op | source)
XLA Modules:
  0.0 121.6 jit_solution(16006095433698673209)
XLA Ops:
  0.6 114.8 %moe_relay.1 = (bf16[128,3584]{1,0:T(8,128)(2,1)}, bf16[128,3584]{1,0:T(8,128)(2,1)}, bf16[896,128]{1,0:T(8,128)(2,1)}, bf16[896,128]{1,0:T(8,128)(2,1)}, bf16[896,128]{1,0:T(8,128)(2,1)}) custom-call(bf16[128,3584]{1,0:T(8,128)(2,1)} %bitcast.18, bf16[128,3584]{1,0:T(8,128)(2,1)} %bitcast.19, s32[8,128]{1,0:T(8,128)} %bitcast.26, f32[8,128]{1,0:T(8,128)} %bitcast.27, ...), custom_call_target="tpu_custom_call" | custom-call | tf_op jit(solution)/shard_map/moe_relay/pallas_call | solution.py:411
  115.4 0.0 copy-start
  115.4 2.2 %copy.17 = bf16[1,128,3584]{2,1,0:T(8,128)(2,1)} copy(bf16[1,128,3584]{2,1,0:T(8,128)(2,1)} %bitcast.17) | data formatting | bytes 1835008
  117.7 0.0 copy-done
  117.7 0.0 copy-start.3
  117.7 0.9 copy.18
  118.6 0.3 copy-done.3
  118.8 0.0 copy-start.2
  118.8 0.7 copy.19
  119.5 0.3 copy-done.2
  119.9 0.0 copy-start.1
  119.9 0.7 copy.20
  120.5 0.3 copy-done.1
  120.9 0.7 copy.21
Async XLA Ops:
  115.4 2.3 %copy-start = (bf16[128,3584]{1,0:T(8,128)(2,1)S(1)}, bf16[128,3584]{1,0:T(8,128)(2,1)}, u32[]{:S(2)}) copy-start(bf16[128,3584]{1,0:T(8,128)(2,1)} %get-tuple-element.11) | copy-start | bytes 2752516
  117.7 1.2 copy-start.3
  118.8 1.0 copy-start.2
  119.9 1.0 copy-start.1
